TPU v7x, 256 devices: a whole 4x4x8 slice. The times are simulated.
256 devices in a mesh: seq: 16 (over y_lo, x, core), head: 16 (over z, y_hi).
Axes of the slice: x: 4, y: 4 (y_hi: 2, y_lo: 2; y = y_hi * 2 + y_lo), z: 8, core: 2. Of those that a mesh axis runs over, the one named last changes fastest.
Arguments:
- queries: bfloat16 [32768, 8192], P(('seq', 'head')), may hold values from -8 to 8
- keys: bfloat16 [32768, 1024], P(('seq', 'head')), may hold values from -4 to 4
- values: bfloat16 [32768, 1024], P(('seq', 'head')), may hold values from -6 to 6
- band_tiles: int32 [64], replicated, may hold values from 1 to 16, as said below
- vertical_tiles: int32 [64, 16], replicated, may hold values from 0 to 255, as said below
- head_order: int32 [64], replicated, may hold values from 0 to 63, as said below
Outputs:
- attention: bfloat16 [32768, 8192], P(('seq', 'head'))
Inputs may be any that keep to these rules, and one draw needn't show every extreme that they name: band_tiles[h] is the width of head h's band in tiles. vertical_tiles[h, g] is a tile of sequence group g: between g * 16 and (g + 1) * 16 - 1. `head_order`: a permutation of the heads; positions d * 4 to (d + 1) * 4 - 1 are the heads that index d of head serves.
All inputs are finite; a program needn't handle non-finite values.
Results may differ from a plain program's by a relative error of at most 0.0049.
Values may be sent and summed in bfloat16 or wider, within the bound.
A program may use at most 128 MiB of HBM per device.

v0:
```python
import jax
import jax.numpy as jnp
from jax import lax
from jax.sharding import PartitionSpec as P

HEADS = 64
KV_HEADS = 8
HD = 128
TILE = 128
SLASH_MAX = 16


NEGATIVE = -1e30


def passed_along(block, axis, distance):
    devices = range(lax.axis_size(axis))
    route = [(i - distance, i) for i in devices if i - distance in devices]
    return lax.ppermute(block, axis, route)


def slice_tile(source, first_row):
    return lax.dynamic_slice_in_dim(source, first_row, TILE, 0)


def attend_slot(
    query_rows,
    key_padded,
    value_padded,
    far_keys,
    far_values,
    band_width,
    far_tile,
    first_tile,
    widest,
):
    row_count = query_rows.shape[0]
    tile_count = row_count // TILE
    factor = HD ** (-0.5)
    query_tiles = query_rows.reshape(tile_count, TILE, HD)
    tile_ids = first_tile + jnp.arange(tile_count, dtype=jnp.int32)
    inside = jnp.arange(TILE)[:, None] >= jnp.arange(TILE)[None, :]

    def band_step(offset, state):
        row_max, row_mass, weighted = state
        first_row = (widest - 1 - offset) * TILE
        key_tiles = lax.dynamic_slice_in_dim(key_padded, first_row, row_count, 0).reshape(
            tile_count, TILE, HD
        )
        value_tiles = lax.dynamic_slice_in_dim(value_padded, first_row, row_count, 0).reshape(
            tile_count, TILE, HD
        )
        scores = (
            jnp.einsum("tqd,tkd->tqk", query_tiles, key_tiles, preferred_element_type=jnp.float32)
            * factor
        )
        usable = (tile_ids - offset >= 0)[:, None, None] & ((offset > 0) | inside)[None]
        scores = jnp.where(usable, scores, NEGATIVE)
        new_max = jnp.maximum(row_max, jnp.max(scores, axis=2))
        weight = jnp.where(usable, jnp.exp(scores - new_max[..., None]), 0.0)
        shrink = jnp.exp(row_max - new_max)
        row_mass = row_mass * shrink + jnp.sum(weight, axis=2)
        weighted = weighted * shrink[..., None] + jnp.einsum(
            "tqk,tkd->tqd",
            weight.astype(jnp.bfloat16),
            value_tiles,
            preferred_element_type=jnp.float32,
        )
        return (new_max, row_mass, weighted)

    start_state = (
        jnp.full((tile_count, TILE), NEGATIVE, jnp.float32),
        jnp.zeros((tile_count, TILE), jnp.float32),
        jnp.zeros((tile_count, TILE, HD), jnp.float32),
    )
    row_max, row_mass, weighted = lax.fori_loop(0, band_width, band_step, start_state)
    block_rows = min(512, row_count)
    block_count = row_count // block_rows
    row_tiles = first_tile + jnp.arange(row_count, dtype=jnp.int32) // TILE

    def finish(pieces):
        query_block, max_block, mass_block, sum_block, tile_block = pieces
        far_scores = (
            jnp.einsum("qd,kd->qk", query_block, far_keys, preferred_element_type=jnp.float32)
            * factor
        )
        usable = far_tile[None, :] <= (tile_block - band_width)[:, None]
        far_scores = jnp.where(usable, far_scores, NEGATIVE)
        new_max = jnp.maximum(max_block, jnp.max(far_scores, axis=1))
        weight = jnp.where(usable, jnp.exp(far_scores - new_max[:, None]), 0.0)
        shrink = jnp.exp(max_block - new_max)
        mass_block = mass_block * shrink + jnp.sum(weight, axis=1)
        sum_block = sum_block * shrink[:, None] + jnp.dot(
            weight.astype(jnp.bfloat16), far_values, preferred_element_type=jnp.float32
        )
        return (sum_block / mass_block[:, None]).astype(jnp.bfloat16)

    result = lax.map(
        finish,
        (
            query_rows.reshape(block_count, block_rows, HD),
            row_max.reshape(block_count, block_rows),
            row_mass.reshape(block_count, block_rows),
            weighted.reshape(block_count, block_rows, HD),
            row_tiles.reshape(block_count, block_rows),
        ),
    )
    return result.reshape(row_count, HD)


def body(queries, keys, values, band_tiles, vertical_tiles, head_order):
    head_count = lax.axis_size("head")
    seq_index = lax.axis_index("seq")
    head_index = lax.axis_index("head")
    tok_rows = queries.shape[0]
    slot_count = HEADS // head_count
    group_rows = tok_rows * head_count
    group_tiles = group_rows // TILE
    widest = min(SLASH_MAX, group_tiles)
    heads_per_kv = HEADS // KV_HEADS
    tail_rows = (widest - 1) * TILE
    my_heads = lax.dynamic_slice_in_dim(head_order, head_index * slot_count, slot_count)
    my_kv = my_heads // heads_per_kv
    query_heads = queries.reshape(tok_rows, HEADS, HD)
    key_local = keys.reshape(tok_rows, KV_HEADS, HD).transpose(1, 0, 2)
    value_local = values.reshape(tok_rows, KV_HEADS, HD).transpose(1, 0, 2)
    sent_queries = (
        jnp.take(query_heads, head_order, axis=1)
        .reshape(tok_rows, head_count, slot_count, HD)
        .transpose(1, 2, 0, 3)
    )
    arrived_queries = lax.all_to_all(sent_queries, "head", split_axis=0, concat_axis=2, tiled=True)
    group_keys, group_values = (
        lax.all_gather(key_local, "head", axis=1, tiled=True),
        lax.all_gather(value_local, "head", axis=1, tiled=True),
    )
    slot_keys = jnp.take(group_keys, my_kv, axis=0)
    slot_values = jnp.take(group_values, my_kv, axis=0)
    tail_pair = jnp.stack(
        [slot_keys[:, group_rows - tail_rows :], slot_values[:, group_rows - tail_rows :]]
    )
    prior_pair = passed_along(tail_pair, "seq", 1)
    tail_keys = prior_pair[0]
    tail_values = prior_pair[1]
    slot_queries = arrived_queries[0]
    key_padded = jnp.concatenate([tail_keys, slot_keys], axis=1)
    value_padded = jnp.concatenate([tail_values, slot_values], axis=1)
    my_vertical = jnp.take(vertical_tiles, my_heads, axis=0)
    own_tile = lax.dynamic_index_in_dim(my_vertical, seq_index, 1, keepdims=False)
    offsets = (own_tile - seq_index * group_tiles) * TILE
    picked_keys = jax.vmap(slice_tile)(slot_keys, offsets)
    picked_values = jax.vmap(slice_tile)(slot_values, offsets)
    far_pair = lax.all_gather(jnp.stack([picked_keys, picked_values]), "seq", axis=2, tiled=True)
    far_tiles = jnp.repeat(my_vertical, TILE, axis=1)
    band_slots = jnp.take(band_tiles, my_heads)
    first_tile = seq_index * group_tiles

    def per_slot(pieces):
        query_rows, keys_slot, values_slot, far_keys, far_values, band_width, far_tile = pieces
        return attend_slot(
            query_rows,
            keys_slot,
            values_slot,
            far_keys,
            far_values,
            band_width,
            far_tile,
            first_tile,
            widest,
        )

    attended = lax.map(
        per_slot,
        (slot_queries, key_padded, value_padded, far_pair[0], far_pair[1], band_slots, far_tiles),
    )
    returned = lax.all_to_all(
        attended.reshape(slot_count, head_count, tok_rows, HD),
        "head",
        split_axis=1,
        concat_axis=1,
        tiled=True,
    )
    return jnp.transpose(returned, (2, 1, 0, 3)).reshape(tok_rows, HEADS * HD)


def solution(mesh):
    placed = (
        P(("seq", "head"), None),
        P(("seq", "head"), None),
        P(("seq", "head"), None),
        P(),
        P(),
        P(),
    )
    return jax.shard_map(
        body, mesh=mesh, in_specs=placed, out_specs=P(("seq", "head"), None), check_vma=False
    )
```

profile of v0, /device:TPU:10, one launch (start us, length us, event | category | flops | bytes accessed | tf_op | source)
XLA Modules:
  0.0 667.3 jit_solution(16978974600455302036)
XLA Ops:
  11.7 100.3 %all-gather.4.cloned.1.call-done = bf16[8,2048,128]{2,1,0:T(8,128)(2,1)} async-done(((bf16[8,128,128]{2,1,0:T(8,128)(2,1)}), bf16[8,2048,128]{2,1,0:T(8,128)(2,1)}) %all-gather.4.cloned.1.call-update) | async-done | bytes 4194320 | tf_op jit(solution)/shard_map/all_gather | solution.py:134
  112.0 4.4 gather_fusion.5
  116.4 94.8 %all-gather.6.cloned.1.call-done = bf16[8,2048,128]{2,1,0:T(8,128)(2,1)} async-done(((bf16[8,128,128]{2,1,0:T(8,128)(2,1)}), bf16[8,2048,128]{2,1,0:T(8,128)(2,1)}) %all-gather.6.cloned.1.call-update) | async-done | bytes 4194320 | tf_op jit(solution)/shard_map/all_gather | solution.py:135
  211.2 4.3 gather_fusion.6
  215.5 2.7 broadcast_select_fusion
  218.2 10.7 %copy.59 = bf16[4,2048,128]{2,0,1:T(4,128)(2,1)} copy(bf16[4,2048,128]{2,1,0:T(8,128)(2,1)S(1)} %get-tuple-element.403) | data formatting | bytes 4194304 | tf_op jit(solution)/shard_map/jit(_take)/select_n | solution.py:137
  228.9 10.7 %copy.60 = bf16[4,2048,128]{2,0,1:T(4,128)(2,1)} copy(bf16[4,2048,128]{2,1,0:T(8,128)(2,1)S(1)} %get-tuple-element.402) | data formatting | bytes 4194304 | tf_op jit(solution)/shard_map/jit(_take)/select_n | solution.py:138
  244.5 4.1 copy.51
  248.6 4.1 copy.52
  252.8 3.9 gather_fusion
  256.7 3.2 select_bitcast_fusion
  259.9 4.9 all-to-all-start
  271.5 41.4 %all-to-all-done = bf16[16,4,128,128]{3,2,1,0:T(8,128)(2,1)} async-done(((bf16[16,4,128,128]{3,2,1,0:T(8,128)(2,1)}), bf16[16,4,128,128]{3,2,1,0:T(8,128)(2,1)}, u32[]{:S(2)}, u32[]{:S(2)}) %all-to-all-start) | async-done | bytes 2097184 | tf_op jit(solution)/shard_map/all_to_all | solution.py:132
  312.9 3.2 copy.53
  316.1 3.7 collective-permute-done
  322.2 3.6 pad_maximum_fusion
  325.8 18.3 %all-gather.8.cloned.1.call-done = bf16[2,4,2048,128]{3,1,2,0:T(4,128)(2,1)} async-done(((bf16[2,4,128,128]{3,1,2,0:T(4,128)(2,1)}), bf16[2,4,2048,128]{3,1,2,0:T(4,128)(2,1)}) %all-gather.8.cloned.1.call-update) | async-done | bytes 4194320 | tf_op jit(solution)/shard_map/all_gather | solution.py:153
  344.1 3.0 slice_bitcast_fusion
  350.3 244.1 %while.63 = (s32[]{:T(128)}, bf16[4,2048,128]{2,1,0:T(8,128)(2,1)}, bf16[4,2048,128]{2,1,0:T(8,128)(2,1)}, s32[4]{0:T(128)S(1)}, bf16[4,3968,128]{2,1,0:T(8,128)...) while((s32[]{:T(128)}, bf16[4,2048,128]{2,1,0:T(8,128)(2,1)}, ...), condition=%wide.region_9.11_spmd, body=%wide.region_0.10_spmd.sunk | while | flops 691873344 | bytes 32720728 | solution.py:172
  355.5 74.5 %while.64 = (s32[]{:T(128)}, f32[16,128]{1,0:T(8,128)S(1)}, f32[16,128]{1,0:T(8,128)S(1)}, f32[16,128,128]{2,1,0:T(8,128)S(1)}, s32[]{:T(128)}, /*index=5*/bf16[...) while((s32[]{:T(128)}, f32[16,128]{1,0:T(8,128)S(1)}, ...), condition=%wide.region_4.5_spmd.clone, body=%wide.region_1.4_spmd.clone.sunk | while | flops 137924672 | bytes 9109781 | solution.py:76
  431.3 21.9 %while.65 = (s32[]{:T(128)}, bf16[4,512,128]{2,1,0:T(8,128)(2,1)S(1)}, f32[4,512,128]{2,1,0:T(8,128)S(1)}, f32[4,512]{1,0:T(4,128)S(1)}, s32[2048]{0:T(1024)S(1)...) while((s32[]{:T(128)}, ...), condition=%wide.region_8.9_spmd, body=%wide.region_5.8_spmd.sunk | while | flops 553911808 | bytes 14230149 | solution.py:98
  459.2 23.7 %while.64 = (s32[]{:T(128)}, f32[16,128]{1,0:T(8,128)S(1)}, f32[16,128]{1,0:T(8,128)S(1)}, f32[16,128,128]{2,1,0:T(8,128)S(1)}, s32[]{:T(128)}, /*index=5*/bf16[...) while((s32[]{:T(128)}, f32[16,128]{1,0:T(8,128)S(1)}, ...), condition=%wide.region_4.5_spmd.clone, body=%wide.region_1.4_spmd.clone.sunk | while | flops 137924672 | bytes 9109781 | solution.py:76
  484.3 21.9 %while.65 = (s32[]{:T(128)}, bf16[4,512,128]{2,1,0:T(8,128)(2,1)S(1)}, f32[4,512,128]{2,1,0:T(8,128)S(1)}, f32[4,512]{1,0:T(4,128)S(1)}, s32[2048]{0:T(1024)S(1)...) while((s32[]{:T(128)}, ...), condition=%wide.region_8.9_spmd, body=%wide.region_5.8_spmd.sunk | while | flops 553911808 | bytes 14230149 | solution.py:98
  507.0 2.6 dynamic-slice_bitcast_fusion.6
  512.2 23.7 %while.64 = (s32[]{:T(128)}, f32[16,128]{1,0:T(8,128)S(1)}, f32[16,128]{1,0:T(8,128)S(1)}, f32[16,128,128]{2,1,0:T(8,128)S(1)}, s32[]{:T(128)}, /*index=5*/bf16[...) while((s32[]{:T(128)}, f32[16,128]{1,0:T(8,128)S(1)}, ...), condition=%wide.region_4.5_spmd.clone, body=%wide.region_1.4_spmd.clone.sunk | while | flops 137924672 | bytes 9109781 | solution.py:76
  537.2 21.9 %while.65 = (s32[]{:T(128)}, bf16[4,512,128]{2,1,0:T(8,128)(2,1)S(1)}, f32[4,512,128]{2,1,0:T(8,128)S(1)}, f32[4,512]{1,0:T(4,128)S(1)}, s32[2048]{0:T(1024)S(1)...) while((s32[]{:T(128)}, ...), condition=%wide.region_8.9_spmd, body=%wide.region_5.8_spmd.sunk | while | flops 553911808 | bytes 14230149 | solution.py:98
  559.9 2.6 dynamic-slice_bitcast_fusion.6
  565.1 5.2 while.64
  571.7 21.9 %while.65 = (s32[]{:T(128)}, bf16[4,512,128]{2,1,0:T(8,128)(2,1)S(1)}, f32[4,512,128]{2,1,0:T(8,128)S(1)}, f32[4,512]{1,0:T(4,128)S(1)}, s32[2048]{0:T(1024)S(1)...) while((s32[]{:T(128)}, ...), condition=%wide.region_8.9_spmd, body=%wide.region_5.8_spmd.sunk | while | flops 553911808 | bytes 14230149 | solution.py:98
  594.4 3.4 copy.63
  597.8 56.5 %all_to_all.20 = bf16[4,16,128,128]{3,0,2,1:T(4,128)(2,1)S(1)} all-to-all(bf16[4,16,128,128]{3,0,2,1:T(4,128)(2,1)S(1)} %bitcast.132), channel_id=1, replica_groups=mesh['seq'=16,'head'=16] {'head'}, dimensions={1} | all-to-all | bytes 4194304 | tf_op jit(solution)/shard_map/all_to_all | solution.py:176
  656.7 4.1 copy.65
  (456 shorter events, 242.7 us)
Async XLA Ops:
  6.5 264.3 %copy-start = (s32[64]{0:T(128)S(1)}, s32[64]{0:T(128)}, u32[]{:S(2)}) copy-start(s32[64]{0:T(128)} %param.17) | copy-start | bytes 772
  6.5 4.2 copy-start.5
  6.5 4.3 copy-start.6
  6.5 105.5 %all-gather.4.cloned.1.call-start = ((), (), s32[]{:S(2)}) async-start(), calls=%async_computation.2 | async-start | bytes 4456448 | tf_op jit(solution)/shard_map/all_gather | solution.py:134
  8.6 202.6 %all-gather.6.cloned.1.call-start = ((), (), s32[]{:S(2)}) async-start(), calls=%async_computation.3 | async-start | bytes 4456448 | tf_op jit(solution)/shard_map/all_gather | solution.py:135
  10.7 333.4 %all-gather.8.cloned.1.call-start = ((), (), s32[]{:S(2)}) async-start(), calls=%async_computation.4 | async-start | bytes 4456448 | tf_op jit(solution)/shard_map/all_gather | solution.py:153
  218.2 10.7 %copy-start.2 = (bf16[4,2048,128]{2,1,0:T(8,128)(2,1)}, bf16[4,2048,128]{2,1,0:T(8,128)(2,1)S(1)}, u32[]{:S(2)}) copy-start(bf16[4,2048,128]{2,1,0:T(8,128)(2,1)S(1)} %get-tuple-element.403) | copy-start | bytes 6291460
  259.9 53.0 %all-to-all-start = ((bf16[16,4,128,128]{3,2,1,0:T(8,128)(2,1)}), bf16[16,4,128,128]{3,2,1,0:T(8,128)(2,1)}, u32[]{:S(2)}, u32[]{:S(2)}) async-start(bf16[16,4,128,128]{3,2,1,0:T(8,128)(2,1)} %select_bitcast_fusion), calls=%async_computation | async-start | bytes 4194304 | tf_op jit(solution)/shard_map/all_to_all | solution.py:132
  264.8 1.6 copy-start.3
  268.8 51.0 %collective-permute-start = (bf16[2,4,1920,128]{3,2,1,0:T(8,128)(2,1)}, bf16[2,4,1920,128]{3,2,1,0:T(8,128)(2,1)}, u32[]{:S(2)}, u32[]{:S(2)}) collective-permute-start(bf16[2,4,1920,128]{3,2,1,0:T(8,128)(2,1)} %pad_maximum_fusion.2), channel_id=1, source_target_pairs={{0,16},{16,32},{32,48},{48,64},{64,80},{80,96},{96,112},{112,128},... | collective-permute-start | bytes 11796488 | tf_op jit(solution)/shard_map/ppermute | solution.py:19
  316.1 6.1 copy-start.4
  656.7 4.1 copy-start.1
Sparse Core Ops, SparseCore 0:
  10.0 102.0 all-gather.3
  114.6 96.5 all-gather.5
  244.7 99.3 all-gather.7
where the time goes:
time: 672 us; the launch traced here: 667 us
  waiting for transfers between devices  259 us (39%)
  local copies, waits for them, and re-layouts  135 us (20%)
  matrix products  125 us (19%)
  blocking collectives  56.5 us (8%)
  other arithmetic  51.1 us (8%)
  loops' own time  21 us (3%)
  between operations  13.3 us (2%)
  starting transfers between devices  6.86 us (1%)
    all_gather x1, waiting for transfers between devices, body(): lax.all_gather(key_local, 'head', axis=1, tiled=True)  100 us
    all_gather x1, waiting for transfers between devices, body(): lax.all_gather(value_local, 'head', axis=1, tiled=True)  94.8 us
    all_to_all x1, blocking collectives, body(): lax.all_to_all(attended.reshape(slot_count, head_count, tok_rows, HD), 'h...  56.5 us
    dot_general x27, matrix products, band_step(): jnp.einsum('tqd,tkd->tqk', query_tiles, key_tiles, preferred_element_type...  41.7 us
    all_to_all x1, waiting for transfers between devices, body(): lax.all_to_all(sent_queries, 'head', split_axis=0, concat_axis=2, tiled=T...  41.4 us
    dynamic_slice x27, local copies, waits for them, and re-layouts, band_step(): lax.dynamic_slice_in_dim(value_padded, first_row, row_count, 0)  30.1 us
    dot_general x16, matrix products, finish(): jnp.einsum('qd,kd->qk', query_block, far_keys, preferred_element_type=jnp...  29.6 us
    dot_general x16, matrix products, finish(): jnp.dot(weight.astype(jnp.bfloat16), far_values, preferred_element_type=j...  27.7 us
  transfers between devices with their start and end apart: 5, of which 5 were waited for; matrix products, arithmetic and copies ran while one was open for 5% of the time, Pallas kernels for 0%

commit v1 on v0

v1 whole, which is shorter than its diff:
```python
import functools

import jax
import jax.numpy as jnp
from jax import lax
from jax.experimental import pallas as pl
from jax.experimental.pallas import tpu as pltpu
from jax.sharding import PartitionSpec as P

HEADS = 64
HD = 128
TILE = 128
MESH = pl.DeviceIdType.MESH
NEG = -1e30
SCALE = 1.4426950408889634 * HD**-0.5
PLUS, MINUS = 0, 1
ARRIVALS = [(d, h) for h in range(1, 5) for d in (PLUS, MINUS)]


def device_id(ylo, x, yhi, z, c):
    return (ylo * 8 + x * 2 + c, z * 2 + yhi)


def kernel(
    band_ref,
    vert_ref,
    order_ref,
    q_ref,
    k_ref,
    v_ref,
    out_ref,
    kvs,
    kv,
    qb,
    far,
    vsel,
    ob,
    orecv,
    sb,
    mx,
    acc,
    den,
    q_ss,
    q_rs,
    a_ss,
    a_rs,
    z_ss,
    z_rs,
    b_ss,
    b_rs,
    f_ss,
    f_rs,
    o_ss,
    o_rs,
    t_s,
    y_s,

):
    seq, jj = lax.axis_index("seq"), lax.axis_index("head")
    ylo, x, c = seq // 8, (seq // 2) % 4, seq % 2
    z, yhi = jj // 2, jj % 2
    me = (x * 2 + yhi) * 2 + c
    kvh = x * 2 + yhi
    my_tile = (x * 2 + c) * 2 + yhi

    def member(o):
        return device_id(ylo, o // 4, (o // 2) % 2, z, o % 2)

    def tile_of(o):
        return ((o // 4) * 2 + o % 2) * 2 + (o // 2) % 2

    up = device_id(ylo, x, yhi, (z + 1) % 8, c)
    down = device_id(ylo, x, yhi, (z + 7) % 8, c)
    twin = device_id(ylo, x, yhi, z, 1 - c)
    across = device_id(1 - ylo, x, yhi, z, c)

    def send(src, dst, ss, rs, dev):
        return pltpu.make_async_remote_copy(
            src_ref=src, dst_ref=dst, send_sem=ss, recv_sem=rs, device_id=dev, device_id_type=MESH
        )

    barrier = pltpu.get_barrier_semaphore()
    for r in range(1, 16):
        pl.semaphore_signal(barrier, inc=1, device_id=member((me + r) % 16), device_id_type=MESH)
    for dev in (up, down, across):
        pl.semaphore_signal(barrier, inc=1, device_id=dev, device_id_type=MESH)

    for g in range(8):
        kvs[g, 0] = k_ref[:, g * HD : (g + 1) * HD]
        kvs[g, 1] = v_ref[:, g * HD : (g + 1) * HD]

    @pl.when(ylo == 0)
    def _():
        kv[0:16] = jnp.zeros((16, 2, TILE, HD), jnp.bfloat16)

    pl.semaphore_wait(barrier, 18)

    here = 16 + (x * 2 + c) * 16 + jj
    for r in range(1, 8):
        g = (kvh + r) % 8
        send(kvs.at[g], kv.at[here], a_ss.at[r], a_rs.at[r], member(g * 2 + c)).start()
    for r in range(1, 16):
        o = (me + r) % 16
        send(
            q_ref.at[:, pl.ds(pl.multiple_of(o * 512, 512), 512)],
            qb.at[my_tile],
            q_ss.at[r],
            q_rs.at[r],
            member(o),
        ).start()
    kv[here] = kvs[kvh]
    qb[my_tile] = q_ref[:, pl.ds(pl.multiple_of(me * 512, 512), 512)]
    for r in range(1, 8):
        g = (kvh + 8 - r) % 8
        at = 16 + ((g // 2) * 2 + c) * 16 + 2 * z + g % 2
        send(kvs.at[0], kv.at[at], a_ss.at[r], a_rs.at[r], twin).wait_recv()

    extra = (ylo == 1) & (c == 1)

    def block(nb, zz):
        first = 2 * zz if nb == 4 else 16 + (nb * 2 + c) * 16 + 2 * zz
        return kv.at[pl.ds(first, 2)]

    def twin_block(nb, zz):
        first = 2 * zz if nb == 4 else 16 + (nb * 2 + 1 - c) * 16 + 2 * zz
        return kv.at[pl.ds(first, 2)]

    def travels(d, h, nb):
        return h < 4 or (d == PLUS) == (nb in (0, 1, 4))

    def origin(d, h):
        return (z + 8 - h) % 8 if d == PLUS else (z + h) % 8

    def ring(d, h, nb):
        blk = block(nb, origin(d, h - 1))
        return send(blk, blk, z_ss.at[d, h - 1, nb], z_rs.at[d, h - 1, nb], up if d == PLUS else down)

    def ring_landing(d, h, nb):
        blk = block(nb, origin(d, h))
        return send(blk, blk, z_ss.at[d, h - 1, nb], z_rs.at[d, h - 1, nb], up if d == PLUS else down)

    def hand(q, nb, zz):
        blk = block(nb, zz)
        return send(blk, blk, b_ss.at[q, nb], b_rs.at[q, nb], twin)

    def handed(q, nb, zz):
        blk = twin_block(nb, zz)
        return send(blk, blk, b_ss.at[q, nb], b_rs.at[q, nb], twin)

    tail_src = kv.at[pl.ds(128 + 2 * z, 2)]
    tail_dst = kv.at[pl.ds(2 * z, 2)]
    tail = send(tail_src, tail_dst, t_s.at[0], t_s.at[1], across)

    @pl.when((ylo == 0) & (c == 1))
    def _():
        tail.start()

    def begin(nb):
        ring(PLUS, 1, nb).start()
        ring(MINUS, 1, nb).start()
        hand(0, nb, z).start()

    for nb in range(4):
        begin(nb)

    @pl.when(extra)
    def _():
        tail.wait_recv()
        begin(4)

    def arrive(q, d, h, nb):
        ring_landing(d, h, nb).wait_recv()
        if h < 4 and travels(d, h + 1, nb):
            ring(d, h + 1, nb).start()
        hand(q + 1, nb, origin(d, h)).start()

    for q, (d, h) in enumerate(ARRIVALS):
        for nb in range(4):
            if travels(d, h, nb):
                arrive(q, d, h, nb)
        if travels(d, h, 4):

            @pl.when(extra)
            def _():
                arrive(q, d, h, 4)

    def each_handed(act):
        for nb in range(5):

            def one():
                act(0, nb, z)
                for q, (d, h) in enumerate(ARRIVALS):
                    if travels(d, h, nb):
                        act(q + 1, nb, origin(d, h))

            yield nb, one

    for nb, one in each_handed(lambda q, nb, zz: handed(q, nb, zz).wait_recv()):
        if nb < 4:
            one()
        else:
            pl.when((ylo == 1) & (c == 0))(one)

    to_upper = send(vsel, far.at[z], y_s.at[0], y_s.at[1], across)

    def far_ring(d, h):
        blk = far.at[origin(d, h - 1)]
        return send(blk, blk, f_ss.at[d, h - 1], f_rs.at[d, h - 1], up if d == PLUS else down)

    def far_landing(d, h):
        blk = far.at[origin(d, h)]
        return send(blk, blk, f_ss.at[d, h - 1], f_rs.at[d, h - 1], up if d == PLUS else down)

    @pl.when(ylo == 0)
    def _():
        for a in range(4):
            vsel[a] = kv[16 + z * 16 + (vert_ref[me * 4 + a, z] & 15)]
        to_upper.start()
        to_upper.wait_send()

    far_hops = [(d, h) for d, h in ARRIVALS if not (d == MINUS and h == 4)]

    @pl.when(ylo == 1)
    def _():
        to_upper.wait_recv()
        far_ring(PLUS, 1).start()
        far_ring(MINUS, 1).start()
        for d, h in far_hops:
            far_landing(d, h).wait_recv()
            if (d, h + 1) in far_hops:
                far_ring(d, h + 1).start()

    def own_far(n, carry):
        g = ylo * 8 + n // 4
        a = n % 4
        far[g, a] = kv[16 + (n // 4) * 16 + (vert_ref[me * 4 + a, g] & 15)]
        return carry

    lax.fori_loop(0, 32, own_far, 0)

    for r in range(1, 16):
        o = (me + 16 - r) % 16
        send(
            q_ref.at[:, pl.ds(0, 512)], qb.at[tile_of(o)], q_ss.at[r], q_rs.at[r], member(o)
        ).wait_recv()

    rows_id = lax.broadcasted_iota(jnp.int32, (TILE, TILE), 0)
    cols_id = lax.broadcasted_iota(jnp.int32, (TILE, TILE), 1)

    def attend(mi, carry):
        gl, yh = mi // 2, mi % 2
        j = 2 * z + yh
        group = ylo * 8 + gl
        t = group * 16 + j
        start = gl * 16 + j + 1
        qs = [qb[mi, :, a * HD : (a + 1) * HD] for a in range(4)]
        q4 = jnp.concatenate(qs, axis=0)
        lims = [jnp.minimum(band_ref[me * 4 + a], t + 1) for a in range(4)]
        chunks = group // 4 + 1

        for cc in range(4):
            keys = kv[pl.ds(start + 4 * cc, 4), 0].reshape(512, HD)
            s = lax.dot_general(q4, keys, (((1,), (1,)), ((), ())), preferred_element_type=jnp.float32)
            for a in range(4):
                for i in range(4):
                    off = 15 - (4 * cc + i)
                    part = s[a * TILE : (a + 1) * TILE, i * TILE : (i + 1) * TILE]
                    if off == 0:
                        part = jnp.where(rows_id >= cols_id, part, NEG)
                    else:
                        part = part + jnp.where(off < lims[a], 0.0, NEG)
                    sb[cc, a * TILE : (a + 1) * TILE, i * TILE : (i + 1) * TILE] = part
                    if cc == 0 and i == 0:
                        mx[a * TILE : (a + 1) * TILE, :] = part
                    else:
                        mx[a * TILE : (a + 1) * TILE, :] = jnp.maximum(
                            mx[a * TILE : (a + 1) * TILE, :], part
                        )

        def far_scores(ch, carry):
            for a in range(4):
                keys = far[pl.ds(4 * ch, 4), a, 0].reshape(512, HD)
                s = lax.dot_general(
                    qs[a], keys, (((1,), (1,)), ((), ())), preferred_element_type=jnp.float32
                )
                for i in range(4):
                    ok = vert_ref[me * 4 + a, 4 * ch + i] <= t - band_ref[me * 4 + a]
                    part = s[:, i * TILE : (i + 1) * TILE] + jnp.where(ok, 0.0, NEG)
                    sb[4 + ch, a * TILE : (a + 1) * TILE, i * TILE : (i + 1) * TILE] = part
                    mx[a * TILE : (a + 1) * TILE, :] = jnp.maximum(
                        mx[a * TILE : (a + 1) * TILE, :], part
                    )
            return carry

        lax.fori_loop(0, chunks, far_scores, 0)

        top = jnp.max(mx[...], axis=1, keepdims=True) * SCALE
        mx[...] = jnp.broadcast_to(top, (512, HD))

        def weights(n, a):
            p = []
            m = mx[a * TILE : (a + 1) * TILE, :]
            total = None
            for i in range(4):
                w = jnp.exp2(sb[n, a * TILE : (a + 1) * TILE, i * TILE : (i + 1) * TILE] * SCALE - m)
                total = w if total is None else total + w
                p.append(w.astype(jnp.bfloat16))
            return jnp.concatenate(p, axis=1), total

        for cc in range(4):
            vals = kv[pl.ds(start + 4 * cc, 4), 1].reshape(512, HD)
            ps = []
            for a in range(4):
                p, total = weights(cc, a)
                ps.append(p)
                rows = slice(a * TILE, (a + 1) * TILE)
                den[rows, :] = total if cc == 0 else den[rows, :] + total
            pv = jnp.dot(jnp.concatenate(ps, axis=0), vals, preferred_element_type=jnp.float32)
            acc[...] = pv if cc == 0 else acc[...] + pv

        def far_values(ch, carry):
            for a in range(4):
                vals = far[pl.ds(4 * ch, 4), a, 1].reshape(512, HD)
                p, total = weights(4 + ch, a)
                rows = slice(a * TILE, (a + 1) * TILE)
                den[rows, :] = den[rows, :] + total
                acc[rows, :] = acc[rows, :] + jnp.dot(p, vals, preferred_element_type=jnp.float32)
            return carry

        lax.fori_loop(0, chunks, far_values, 0)
        res = acc[...] / jnp.sum(den[...], axis=1, keepdims=True)
        for a in range(4):
            ob[mi, a] = res[a * TILE : (a + 1) * TILE].astype(jnp.bfloat16)

        @pl.when(mi == my_tile)
        def _():
            orecv[pl.ds(me * 4, 4)] = ob[mi]

        @pl.when(mi != my_tile)
        def _():
            send(ob.at[mi], orecv.at[pl.ds(me * 4, 4)], o_ss.at[mi], o_rs.at[me], device_id(ylo, gl // 2, yh, z, gl % 2)).start()

        return carry

    lax.fori_loop(0, 16, attend, 0)

    for r in range(1, 16):
        o = (me + r) % 16
        send(ob.at[0], orecv.at[pl.ds(o * 4, 4)], o_ss.at[tile_of(o)], o_rs.at[o], member(o)).wait_recv()

    for p in range(HEADS):
        out_ref[:, p * HD : (p + 1) * HD] = orecv[order_ref[p]]

    for r in range(1, 8):
        send(kvs.at[0], kv.at[here], a_ss.at[r], a_rs.at[r], twin).wait_send()
    for r in range(1, 16):
        o = (me + r) % 16
        send(q_ref.at[:, pl.ds(0, 512)], qb.at[my_tile], q_ss.at[r], q_rs.at[r], twin).wait_send()
        send(ob.at[0], orecv.at[pl.ds(me * 4, 4)], o_ss.at[tile_of(o)], o_rs.at[me], twin).wait_send()

    @pl.when((ylo == 0) & (c == 1))
    def _():
        tail.wait_send()

    for nb, one in each_handed(lambda q, nb, zz: hand(q, nb, zz).wait_send()):
        if nb < 4:
            one()
        else:
            pl.when(extra)(one)

    def ring_sent(nb):
        for d, h in ARRIVALS:
            if travels(d, h, nb):
                ring(d, h, nb).wait_send()

    for nb in range(4):
        ring_sent(nb)
    pl.when(extra)(functools.partial(ring_sent, 4))

    @pl.when(ylo == 1)
    def _():
        for d, h in far_hops:
            far_ring(d, h).wait_send()


def body(queries, keys, values, band_tiles, vertical_tiles, head_order):
    dma = pltpu.SemaphoreType.DMA
    vm = pl.BlockSpec(memory_space=pltpu.VMEM)
    sm = pl.BlockSpec(memory_space=pltpu.SMEM)
    bf, f32 = jnp.bfloat16, jnp.float32
    return pl.pallas_call(
        kernel,
        out_shape=jax.ShapeDtypeStruct((TILE, HEADS * HD), bf),
        in_specs=[sm, sm, sm, vm, vm, vm],
        out_specs=vm,
        scratch_shapes=[
            pltpu.VMEM((8, 2, TILE, HD), bf),
            pltpu.VMEM((144, 2, TILE, HD), bf),
            pltpu.VMEM((16, TILE, 512), bf),
            pltpu.VMEM((16, 4, 2, TILE, HD), bf),
            pltpu.VMEM((4, 2, TILE, HD), bf),
            pltpu.VMEM((16, 4, TILE, HD), bf),
            pltpu.VMEM((HEADS, TILE, HD), bf),
            pltpu.VMEM((8, 512, 512), f32),
            pltpu.VMEM((512, HD), f32),
            pltpu.VMEM((512, HD), f32),
            pltpu.VMEM((512, HD), f32),
            dma((16,)),
            dma((16,)),
            dma((8,)),
            dma((8,)),
            dma((2, 4, 5)),
            dma((2, 4, 5)),
            dma((9, 5)),
            dma((9, 5)),
            dma((2, 4)),
            dma((2, 4)),
            dma((16,)),
            dma((16,)),
            dma((2,)),
            dma((2,)),

        ],
        compiler_params=pltpu.CompilerParams(
            collective_id=0, has_side_effects=True, vmem_limit_bytes=58 * 2**20
        ),
        name="attention",
    )(band_tiles, vertical_tiles, head_order, queries, keys, values)


def solution(mesh):
    tokens = P(("seq", "head"), None)
    return jax.shard_map(
        body,
        mesh=mesh,
        in_specs=(tokens, tokens, tokens, P(), P(), P()),
        out_specs=tokens,
        check_vma=False,
    )
```

time: 672 us -> 187 us (0.28)
  the two profiles are of different devices: /device:TPU:10 before, /device:TPU:31 now
where the time goes in v1:
time: 187 us
  Pallas kernels  182 us (97%)
  local copies, waits for them, and re-layouts  4.49 us (2%)
    pallas_call x1, Pallas kernels, body(): pl.pallas_call(kernel, out_shape=jax.ShapeDtypeStruct((TILE, HEADS * HD),...  182 us
    unnamed x2, local copies, waits for them, and re-layouts  4.49 us

profile of v1, /device:TPU:31, one launch (start us, length us, event | category | flops | bytes accessed | tf_op | source)
XLA Modules:
  0.0 186.9 jit_solution(6302340837126769484)
XLA Ops:
  0.0 1.4 copy.7.vert_ref
  1.4 182.4 %attention.1 = bf16[128,8192]{1,0:T(8,128)(2,1)} custom-call(s32[64]{0:T(128)} %band_ref.1, s32[64,16]{1,0:T(8,128)} %copy.7.vert_ref, s32[64]{0:T(128)} %order_ref.1, bf16[128,8192]{1,0:T(8,128)(2,1)} %q_ref.1, bf16[128,1024]{1,0:T(8,128)(2,1)} %k_ref.1, bf16[128,1024]{1,0:T(8,128)(2,1)} %v_ref.1), custom_call_target="tpu_custom_call" | custom-call | tf_op jit(solution)/shard_map/attention/pallas_call | solution.py:391
  183.8 3.1 %copy.9 = bf16[128,8192]{1,0:T(8,128)(2,1)} copy(bf16[128,8192]{1,0:T(8,128)(2,1)} %attention.1) | data formatting | bytes 4194304

commit v2 on v1

v2 whole, which is shorter than its diff:
```python
import functools

import jax
import jax.numpy as jnp
from jax import lax
from jax.experimental import pallas as pl
from jax.experimental.pallas import tpu as pltpu
from jax.sharding import PartitionSpec as P

HEADS = 64
HD = 128
TILE = 128
MESH = pl.DeviceIdType.MESH
NEG = -1e30
SCALE = 1.4426950408889634 * HD**-0.5
PLUS, MINUS = 0, 1
ARRIVALS = [(d, h) for h in range(1, 5) for d in (PLUS, MINUS)]


def device_id(ylo, x, yhi, z, c):
    return (ylo * 8 + x * 2 + c, z * 2 + yhi)


def kernel(
    band_ref,
    vert_ref,
    order_ref,
    q_ref,
    k_ref,
    v_ref,
    out_ref,
    kvs,
    kv,
    qb,
    far,
    ob,
    orecv,
    sb,
    mx,
    acc1,
    den1,
    top1,
    q_ss,
    q_rs,
    a_ss,
    a_rs,
    z_ss,
    z_rs,
    b_ss,
    b_rs,
    y_ss,
    y_rs,
    f_ss,
    f_rs,
    o_ss,
    o_rs,
    t_s,
):
    seq, jj = lax.axis_index("seq"), lax.axis_index("head")
    ylo, x, c = seq // 8, (seq // 2) % 4, seq % 2
    z, yhi = jj // 2, jj % 2
    me = (x * 2 + yhi) * 2 + c
    kvh = x * 2 + yhi
    my_tile = (x * 2 + c) * 2 + yhi
    lower, upper = ylo == 0, ylo == 1
    extra = upper & (c == 1)
    f32, bf = jnp.float32, jnp.bfloat16
    rows = [slice(a * TILE, (a + 1) * TILE) for a in range(4)]

    def member(o):
        return device_id(ylo, o // 4, (o // 2) % 2, z, o % 2)

    def tile_of(o):
        return ((o // 4) * 2 + o % 2) * 2 + (o // 2) % 2

    def holder(mi):
        return device_id(ylo, mi // 4, mi % 2, z, (mi // 2) % 2)

    up = device_id(ylo, x, yhi, (z + 1) % 8, c)
    down = device_id(ylo, x, yhi, (z + 7) % 8, c)
    twin = device_id(ylo, x, yhi, z, 1 - c)
    across = device_id(1 - ylo, x, yhi, z, c)
    way = (up, down)

    def send(src, dst, ss, rs, dev):
        return pltpu.make_async_remote_copy(
            src_ref=src, dst_ref=dst, send_sem=ss, recv_sem=rs, device_id=dev, device_id_type=MESH
        )

    barrier = pltpu.get_barrier_semaphore()
    for r in range(1, 16):
        pl.semaphore_signal(barrier, inc=1, device_id=member((me + r) % 16), device_id_type=MESH)
    for dev in (up, down, across):
        pl.semaphore_signal(barrier, inc=1, device_id=dev, device_id_type=MESH)

    for g in range(8):
        kvs[g, 0] = k_ref[:, g * HD : (g + 1) * HD]
        kvs[g, 1] = v_ref[:, g * HD : (g + 1) * HD]

    @pl.when(lower)
    def _():
        kv[0:16] = jnp.zeros((16, 2, TILE, HD), bf)

    far[pl.ds(ylo * 8, 8)] = jnp.zeros((8, 4, 2, TILE, HD), bf)
    pl.semaphore_wait(barrier, 18)

    here = 16 + (x * 2 + c) * 16 + jj
    for r in range(1, 8):
        g = (kvh + r) % 8
        send(kvs.at[g], kv.at[here], a_ss.at[r], a_rs.at[kvh], member(g * 2 + c)).start()
    kv[here] = kvs[kvh]

    def q_send(r):
        o = (me + r) % 16
        return send(
            q_ref.at[:, pl.ds(pl.multiple_of(o * 512, 512), 512)],
            qb.at[my_tile],
            q_ss.at[r],
            q_rs.at[my_tile],
            member(o),
        )

    for r in range(1, 16):
        q_send(r).start()
    qb[my_tile] = q_ref[:, pl.ds(pl.multiple_of(me * 512, 512), 512)]

    def kv_landed(n):
        for yh in range(2):
            g = n * 2 + yh

            @pl.when(kvh != g)
            def _():
                at = 16 + (n * 2 + c) * 16 + 2 * z + yh
                send(kvs.at[0], kv.at[at], a_ss.at[1], a_rs.at[g], twin).wait_recv()

    def first_of(n, core, zz):
        return jnp.where(n == 4, 2 * zz, 16 + (n * 2 + core) * 16 + 2 * zz)

    def block(n, zz):
        return kv.at[pl.ds(first_of(n, c, zz), 2)]

    def origin(d, h):
        return (z + 8 - h) % 8 if d == PLUS else (z + h) % 8

    def goes(d, h, n):
        last = (n < 2) | (n == 4)
        return (h < 4) | (last if d == PLUS else jnp.logical_not(last))

    def ring(d, h, n):
        blk = block(n, origin(d, h - 1))
        return send(blk, blk, z_ss.at[d, h - 1, n], z_rs.at[d, h - 1, n], way[d])

    def ring_landing(d, h, n):
        blk = block(n, origin(d, h))
        return send(blk, blk, z_ss.at[d, h - 1, n], z_rs.at[d, h - 1, n], way[d])

    def slot(d, h):
        return 1 + (h - 1) * 2 + d

    def hand(q, n, zz):
        blk = block(n, zz)
        return send(blk, blk, b_ss.at[q, n], b_rs.at[q, n], twin)

    def handed(q, n, zz):
        blk = kv.at[pl.ds(first_of(n, 1 - c, zz), 2)]
        return send(blk, blk, b_ss.at[q, n], b_rs.at[q, n], twin)

    def begin(n):
        ring(PLUS, 1, n).start()
        ring(MINUS, 1, n).start()
        hand(0, n, z).start()

    def hop(n, h):
        for d in (PLUS, MINUS):

            @pl.when(goes(d, h, n))
            def _():
                ring_landing(d, h, n).wait_recv()

                @pl.when((h < 4) & goes(d, h + 1, n))
                def _():
                    ring(d, jnp.minimum(h + 1, 4), n).start()

                hand(slot(d, h), n, origin(d, h)).start()

    def every(n, act):
        act(0, n, z)
        for d, h in ARRIVALS:
            pl.when(goes(d, h, n))(functools.partial(act, slot(d, h), n, origin(d, h)))

    tail_src = kv.at[pl.ds(128 + 2 * z, 2)]
    tail_dst = kv.at[pl.ds(2 * z, 2)]
    tail = send(tail_src, tail_dst, t_s.at[0], t_s.at[1], across)

    kv_landed(0)
    begin(0)
    kv_landed(3)

    @pl.when(lower & (c == 1))
    def _():
        tail.start()

    kv_landed(1)
    kv_landed(2)

    @pl.when(extra)
    def _():
        tail.wait_recv()
        begin(4)

    hop(0, 1)
    begin(1)
    hop(0, 2)
    pl.when(extra)(functools.partial(hop, 4, 1))
    hop(0, 3)
    hop(1, 1)
    pl.when(extra)(functools.partial(hop, 4, 2))
    begin(2)
    hop(0, 4)
    hop(1, 2)
    pl.when(extra)(functools.partial(hop, 4, 3))
    pl.when(extra)(functools.partial(hop, 4, 4))
    pl.when(upper & (c == 0))(
        functools.partial(every, 4, lambda q, n, zz: handed(q, n, zz).wait_recv())
    )

    def pick(n):
        def one(e, carry):
            g, a = 2 * n + e // 4, e % 4
            want = vert_ref[me * 4 + a, ylo * 8 + g] & 15
            got = kv[16 + g * 16]
            for r in range(1, 16):
                got = jnp.where(want == r, kv[16 + g * 16 + r], got)
            far[ylo * 8 + g, a] = got
            return carry

        lax.fori_loop(0, 8, one, 0)

    def to_upper(n):
        blk = far.at[2 * n + z % 2]
        return send(blk, blk, y_ss.at[n], y_rs.at[n], across)

    def share(n, d, odd):
        blk = far.at[2 * n + odd, pl.ds(2 * d, 2)]
        return send(blk, blk, f_ss.at[n, d], f_rs.at[n, d], way[d])

    rows_id = lax.broadcasted_iota(jnp.int32, (TILE, TILE), 0)
    cols_id = lax.broadcasted_iota(jnp.int32, (TILE, TILE), 1)
    ones = jnp.ones((512, HD), bf)

    def put_scores(cc, a, parts):
        m = None
        for i in range(4):
            sb[cc, rows[a], rows[i]] = parts[i]
            m = parts[i] if m is None else jnp.maximum(m, parts[i])
        mx[cc, rows[a], :] = m

    def far_scores(cc, first, t, qs):
        for a in range(4):
            keys = far[pl.ds(first, 4), a, 0].reshape(512, HD)
            s = lax.dot_general(qs[a], keys, (((1,), (1,)), ((), ())), preferred_element_type=f32)
            parts = []
            for i in range(4):
                ok = vert_ref[me * 4 + a, first + i] <= t - band_ref[me * 4 + a]
                parts.append(s[:, rows[i]] + jnp.where(ok, 0.0, NEG))
            put_scores(cc, a, parts)

    def row_top(n, a):
        m = mx[0, rows[a], :]
        for cc in range(1, n):
            m = jnp.maximum(m, mx[cc, rows[a], :])
        return jnp.max(m, axis=1, keepdims=True) * SCALE

    def weights(cc, a, top):
        return jnp.concatenate(
            [jnp.exp2(sb[cc, rows[a], rows[i]] * SCALE - top).astype(bf) for i in range(4)], axis=1
        )

    def far_sums(cc, first, a, top):
        vals = jnp.concatenate([far[pl.ds(first, 4), a, 1].reshape(512, HD), ones], axis=1)
        return jnp.dot(weights(cc, a, top), vals, preferred_element_type=f32)

    def send_out(mi):
        @pl.when(mi == my_tile)
        def _():
            orecv[pl.ds(me * 4, 4)] = ob[mi]

        @pl.when(mi != my_tile)
        def _():
            send(ob.at[mi], orecv.at[pl.ds(me * 4, 4)], o_ss.at[mi], o_rs.at[me], holder(mi)).start()

    def place(mi):
        gl = mi // 2
        j = 2 * z + mi % 2
        return (ylo * 8 + gl) * 16 + j, gl * 16 + j + 1

    def queries_of(mi):
        return [qb[mi, :, rows[a]] for a in range(4)]

    def attend(mi, carry):
        n, k = mi // 4, mi % 4

        @pl.when((k == 0) & (n < 3))
        def _():
            hop(n + 1, 3)

        @pl.when((k == 1) & (n < 2))
        def _():
            hop(n + 2, 1)

        @pl.when((k == 2) & (n < 3))
        def _():
            hop(n + 1, 4)

        @pl.when((k == 2) & (n < 1))
        def _():
            begin(n + 3)

        @pl.when((k == 3) & (n < 2))
        def _():
            hop(n + 2, 2)

        @pl.when(k == 0)
        def _():
            every(n, lambda q, m, zz: handed(q, m, zz).wait_recv())
            pick(n)

            @pl.when(lower)
            def _():
                to_upper(n).start()

        @pl.when((k == 3) & upper)
        def _():
            to_upper(n).wait_recv()
            share(n, PLUS, z % 2).start()
            share(n, MINUS, z % 2).start()

        @pl.when(mi != my_tile)
        def _():
            send(q_ref.at[:, pl.ds(0, 512)], qb.at[mi], q_ss.at[1], q_rs.at[mi], twin).wait_recv()

        t, start = place(mi)
        qs = queries_of(mi)
        q4 = jnp.concatenate(qs, axis=0)
        lims = [jnp.minimum(band_ref[me * 4 + a], t + 1) for a in range(4)]
        for cc in range(4):
            keys = kv[pl.ds(start + 4 * cc, 4), 0].reshape(512, HD)
            s = lax.dot_general(q4, keys, (((1,), (1,)), ((), ())), preferred_element_type=f32)
            for a in range(4):
                parts = []
                for i in range(4):
                    off = 15 - (4 * cc + i)
                    part = s[rows[a], rows[i]]
                    if off == 0:
                        part = jnp.where(rows_id >= cols_id, part, NEG)
                    else:
                        part = part + jnp.where(off < lims[a], 0.0, NEG)
                    parts.append(part)
                put_scores(cc, a, parts)
        for ch in range(2):
            far_scores(4 + ch, ylo * 8 + 4 * ch, t, qs)

        @pl.when(mi >= 0)
        def _():
            tops = [row_top(6, a) for a in range(4)]
            acc = [None] * 4
            for cc in range(4):
                vals = jnp.concatenate([kv[pl.ds(start + 4 * cc, 4), 1].reshape(512, HD), ones], axis=1)
                p = jnp.concatenate([weights(cc, a, tops[a]) for a in range(4)], axis=0)
                pv = jnp.dot(p, vals, preferred_element_type=f32)
                for a in range(4):
                    acc[a] = pv[rows[a]] if cc == 0 else acc[a] + pv[rows[a]]
            for ch in range(2):
                for a in range(4):
                    acc[a] = acc[a] + far_sums(4 + ch, ylo * 8 + 4 * ch, a, tops[a])
            for a in range(4):
                acc1[mi, rows[a], :] = acc[a][:, :HD]
                den1[mi, rows[a], :] = acc[a][:, HD:]
                top1[mi, rows[a], :] = jnp.broadcast_to(tops[a], (TILE, HD))

        @pl.when(lower)
        def _():
            for a in range(4):
                ob[mi, a] = (acc1[mi, rows[a], :] / den1[mi, rows[a], :]).astype(bf)
            send_out(mi)

        return carry

    lax.fori_loop(0, 16, attend, 0)

    def attend_lower_groups(mi, carry):
        t, _ = place(mi)
        qs = queries_of(mi)
        for ch in range(2):
            far_scores(ch, 4 * ch, t, qs)

        @pl.when(mi >= 0)
        def _():
            for a in range(4):
                old = top1[mi, rows[a], :]
                top = jnp.maximum(row_top(2, a), old)
                keep = jnp.exp2(old - top)
                pv = far_sums(0, 0, a, top) + far_sums(1, 4, a, top)
                num = acc1[mi, rows[a], :] * keep + pv[:, :HD]
                mass = den1[mi, rows[a], :] * keep + pv[:, HD:]
                ob[mi, a] = (num / mass).astype(bf)

        send_out(mi)
        return carry

    @pl.when(upper)
    def _():
        for n in range(4):
            for d in (PLUS, MINUS):
                share(n, d, 1 - z % 2).wait_recv()
        lax.fori_loop(0, 16, attend_lower_groups, 0)

    for r in range(1, 16):
        o = (me + r) % 16
        send(ob.at[0], orecv.at[pl.ds(o * 4, 4)], o_ss.at[tile_of(o)], o_rs.at[o], member(o)).wait_recv()

    for p in range(HEADS):
        out_ref[:, p * HD : (p + 1) * HD] = orecv[order_ref[p]]

    for r in range(1, 8):
        send(kvs.at[0], kv.at[here], a_ss.at[r], a_rs.at[0], twin).wait_send()
    for r in range(1, 16):
        o = (me + r) % 16
        q_send(r).wait_send()
        send(ob.at[0], orecv.at[pl.ds(me * 4, 4)], o_ss.at[tile_of(o)], o_rs.at[me], twin).wait_send()

    @pl.when(lower & (c == 1))
    def _():
        tail.wait_send()

    def sent(n):
        every(n, lambda q, m, zz: hand(q, m, zz).wait_send())
        for d, h in ARRIVALS:
            pl.when(goes(d, h, n))(lambda d=d, h=h: ring(d, h, n).wait_send())

    def sent_in_loop(n, carry):
        sent(n)

        @pl.when(lower)
        def _():
            to_upper(n).wait_send()

        @pl.when(upper)
        def _():
            share(n, PLUS, z % 2).wait_send()
            share(n, MINUS, z % 2).wait_send()

        return carry

    lax.fori_loop(0, 4, sent_in_loop, 0)
    pl.when(extra)(functools.partial(sent, 4))


def body(queries, keys, values, band_tiles, vertical_tiles, head_order):
    dma = pltpu.SemaphoreType.DMA
    vm = pl.BlockSpec(memory_space=pltpu.VMEM)
    sm = pl.BlockSpec(memory_space=pltpu.SMEM)
    bf, f32 = jnp.bfloat16, jnp.float32
    return pl.pallas_call(
        kernel,
        out_shape=jax.ShapeDtypeStruct((TILE, HEADS * HD), bf),
        in_specs=[sm, sm, sm, vm, vm, vm],
        out_specs=vm,
        scratch_shapes=[
            pltpu.VMEM((8, 2, TILE, HD), bf),
            pltpu.VMEM((144, 2, TILE, HD), bf),
            pltpu.VMEM((16, TILE, 512), bf),
            pltpu.VMEM((16, 4, 2, TILE, HD), bf),
            pltpu.VMEM((16, 4, TILE, HD), bf),
            pltpu.VMEM((HEADS, TILE, HD), bf),
            pltpu.VMEM((6, 512, 512), f32),
            pltpu.VMEM((6, 512, HD), f32),
            pltpu.VMEM((16, 512, HD), f32),
            pltpu.VMEM((16, 512, HD), f32),
            pltpu.VMEM((16, 512, HD), f32),
            dma((16,)),
            dma((16,)),
            dma((8,)),
            dma((8,)),
            dma((2, 4, 5)),
            dma((2, 4, 5)),
            dma((9, 5)),
            dma((9, 5)),
            dma((4,)),
            dma((4,)),
            dma((4, 2)),
            dma((4, 2)),
            dma((16,)),
            dma((16,)),
            dma((2,)),
        ],
        compiler_params=pltpu.CompilerParams(
            collective_id=0, has_side_effects=True, vmem_limit_bytes=60 * 2**20
        ),
        name="attention",
    )(band_tiles, vertical_tiles, head_order, queries, keys, values)


def solution(mesh):
    tokens = P(("seq", "head"), None)
    return jax.shard_map(
        body,
        mesh=mesh,
        in_specs=(tokens, tokens, tokens, P(), P(), P()),
        out_specs=tokens,
        check_vma=False,
    )
```

time: 187 us -> 154 us (0.82)
  Pallas kernels: 182 us -> 150 us
    pallas_call x1, Pallas kernels: 182 us -> 150 us  [body(): pl.pallas_call(kernel, out_shape=jax.ShapeDtypeStruct((TILE, HEADS * HD),...]
where the time goes in v2:
time: 154 us
  Pallas kernels  150 us (97%)
  local copies, waits for them, and re-layouts  4.49 us (3%)
    pallas_call x1, Pallas kernels, body(): pl.pallas_call(kernel, out_shape=jax.ShapeDtypeStruct((TILE, HEADS * HD),...  150 us
    unnamed x2, local copies, waits for them, and re-layouts  4.49 us

profile of v2, /device:TPU:31, one launch (start us, length us, event | category | flops | bytes accessed | tf_op | source)
XLA Modules:
  0.0 154.1 jit_solution(16969927675536049463)
XLA Ops:
  0.0 1.4 copy.7.vert_ref
  1.4 149.6 %attention.1 = bf16[128,8192]{1,0:T(8,128)(2,1)} custom-call(s32[64]{0:T(128)} %band_ref.1, s32[64,16]{1,0:T(8,128)} %copy.7.vert_ref, s32[64]{0:T(128)} %order_ref.1, bf16[128,8192]{1,0:T(8,128)(2,1)} %q_ref.1, bf16[128,1024]{1,0:T(8,128)(2,1)} %k_ref.1, bf16[128,1024]{1,0:T(8,128)(2,1)} %v_ref.1), custom_call_target="tpu_custom_call" | custom-call | tf_op jit(solution)/shard_map/attention/pallas_call | solution.py:464
  151.0 3.1 %copy.9 = bf16[128,8192]{1,0:T(8,128)(2,1)} copy(bf16[128,8192]{1,0:T(8,128)(2,1)} %attention.1) | data formatting | bytes 4194304

commit v3 on v2

--- a/solution.py
+++ b/solution.py
@@ -15,6 +15,10 @@
 SCALE = 1.4426950408889634 * HD**-0.5
 PLUS, MINUS = 0, 1
 ARRIVALS = [(d, h) for h in range(1, 5) for d in (PLUS, MINUS)]
+
+CHIPS = [(1, 0), (3, 0), (0, 1), (2, 0), (1, 1), (3, 1), (2, 1)]
+PEERS = [(dx, dy, dc) for dy, dc in ((1, 0), (1, 1), (0, 1), (0, 0)) for dx in (1, 3, 0, 2)]
+PEERS.remove((0, 0, 0))
 
 
 def device_id(ylo, x, yhi, z, c):
@@ -105,13 +109,14 @@
     pl.semaphore_wait(barrier, 18)
 
     here = 16 + (x * 2 + c) * 16 + jj
-    for r in range(1, 8):
-        g = (kvh + r) % 8
+    for r, (dx, dy) in enumerate(CHIPS):
+        g = ((x + dx) % 4) * 2 + (yhi + dy) % 2
         send(kvs.at[g], kv.at[here], a_ss.at[r], a_rs.at[kvh], member(g * 2 + c)).start()
     kv[here] = kvs[kvh]
 
     def q_send(r):
-        o = (me + r) % 16
+        dx, dy, dc = PEERS[r - 1]
+        o = (((x + dx) % 4) * 2 + (yhi + dy) % 2) * 2 + (c + dc) % 2
         return send(
             q_ref.at[:, pl.ds(pl.multiple_of(o * 512, 512), 512)],
             qb.at[my_tile],
@@ -120,8 +125,6 @@
             member(o),
         )
 
-    for r in range(1, 16):
-        q_send(r).start()
     qb[my_tile] = q_ref[:, pl.ds(pl.multiple_of(me * 512, 512), 512)]
 
     def kv_landed(n):
@@ -194,35 +197,29 @@
 
     kv_landed(0)
     begin(0)
+    for r in range(1, 16):
+        q_send(r).start()
+    kv_landed(1)
+    begin(1)
+    hop(0, 1)
+    kv_landed(2)
+    begin(2)
+    hop(0, 2)
+    hop(1, 1)
     kv_landed(3)
+    begin(3)
 
     @pl.when(lower & (c == 1))
     def _():
         tail.start()
 
-    kv_landed(1)
-    kv_landed(2)
-
-    @pl.when(extra)
-    def _():
-        tail.wait_recv()
-        begin(4)
-
-    hop(0, 1)
-    begin(1)
-    hop(0, 2)
-    pl.when(extra)(functools.partial(hop, 4, 1))
     hop(0, 3)
-    hop(1, 1)
-    pl.when(extra)(functools.partial(hop, 4, 2))
-    begin(2)
+    hop(1, 2)
+    hop(2, 1)
     hop(0, 4)
-    hop(1, 2)
-    pl.when(extra)(functools.partial(hop, 4, 3))
-    pl.when(extra)(functools.partial(hop, 4, 4))
-    pl.when(upper & (c == 0))(
-        functools.partial(every, 4, lambda q, n, zz: handed(q, n, zz).wait_recv())
-    )
+    hop(1, 3)
+    hop(2, 2)
+    hop(3, 1)
 
     def pick(n):
         def one(e, carry):
@@ -297,31 +294,44 @@
     def queries_of(mi):
         return [qb[mi, :, rows[a]] for a in range(4)]
 
-    def attend(mi, carry):
-        n, k = mi // 4, mi % 4
-
-        @pl.when((k == 0) & (n < 3))
-        def _():
-            hop(n + 1, 3)
-
-        @pl.when((k == 1) & (n < 2))
-        def _():
-            hop(n + 2, 1)
-
-        @pl.when((k == 2) & (n < 3))
-        def _():
-            hop(n + 1, 4)
-
-        @pl.when((k == 2) & (n < 1))
-        def _():
-            begin(n + 3)
-
-        @pl.when((k == 3) & (n < 2))
-        def _():
-            hop(n + 2, 2)
-
-        @pl.when(k == 0)
-        def _():
+    def attend_lower_groups(pos, carry):
+        dx, u = (1 + 2 * (pos % 4)) % 5, pos // 4
+        dc, dy = ((u + 1) // 2) % 2, 1 - u // 2
+        mi = (((x + dx) % 4) * 2 + (c + dc) % 2) * 2 + (yhi + dy) % 2
+        t, _ = place(mi)
+        qs = queries_of(mi)
+        for ch in range(2):
+            far_scores(ch, 4 * ch, t, qs)
+
+        @pl.when(mi >= 0)
+        def _():
+            for a in range(4):
+                old = top1[mi, rows[a], :]
+                top = jnp.maximum(row_top(2, a), old)
+                keep = jnp.exp2(old - top)
+                pv = far_sums(0, 0, a, top) + far_sums(1, 4, a, top)
+                num = acc1[mi, rows[a], :] * keep + pv[:, :HD]
+                mass = den1[mi, rows[a], :] * keep + pv[:, HD:]
+                ob[mi, a] = (num / mass).astype(bf)
+
+        send_out(mi)
+        return carry
+
+    def start_tail():
+        tail.wait_recv()
+        begin(4)
+
+    def attend(it, carry):
+        mi = (((it + 2) // 2) % 8) * 2 + (it + yhi) % 2
+        for at, (n, h) in enumerate(((1, 4), (2, 3), (3, 2), (2, 4), (3, 3), (3, 4))):
+            pl.when(it == at)(functools.partial(hop, n, h))
+        pl.when(extra & (it == 5))(start_tail)
+        for h in range(1, 5):
+            pl.when(extra & (it == 5 + h))(functools.partial(hop, 4, h))
+
+        @pl.when((it == 0) | (it == 2) | (it == 5) | (it == 7))
+        def _():
+            n = (3 * it + 1) // 7
             every(n, lambda q, m, zz: handed(q, m, zz).wait_recv())
             pick(n)
 
@@ -329,11 +339,16 @@
             def _():
                 to_upper(n).start()
 
-        @pl.when((k == 3) & upper)
-        def _():
+        @pl.when(upper & ((it == 4) | (it == 6) | (it == 9) | (it == 11)))
+        def _():
+            n = (3 * it - 11) // 7
             to_upper(n).wait_recv()
             share(n, PLUS, z % 2).start()
             share(n, MINUS, z % 2).start()
+
+        pl.when(upper & (c == 0) & (it == 14))(
+            functools.partial(every, 4, lambda q, n, zz: handed(q, n, zz).wait_recv())
+        )
 
         @pl.when(mi != my_tile)
         def _():
@@ -388,26 +403,6 @@
 
     lax.fori_loop(0, 16, attend, 0)
 
-    def attend_lower_groups(mi, carry):
-        t, _ = place(mi)
-        qs = queries_of(mi)
-        for ch in range(2):
-            far_scores(ch, 4 * ch, t, qs)
-
-        @pl.when(mi >= 0)
-        def _():
-            for a in range(4):
-                old = top1[mi, rows[a], :]
-                top = jnp.maximum(row_top(2, a), old)
-                keep = jnp.exp2(old - top)
-                pv = far_sums(0, 0, a, top) + far_sums(1, 4, a, top)
-                num = acc1[mi, rows[a], :] * keep + pv[:, :HD]
-                mass = den1[mi, rows[a], :] * keep + pv[:, HD:]
-                ob[mi, a] = (num / mass).astype(bf)
-
-        send_out(mi)
-        return carry
-
     @pl.when(upper)
     def _():
         for n in range(4):
@@ -415,6 +410,7 @@
                 share(n, d, 1 - z % 2).wait_recv()
         lax.fori_loop(0, 16, attend_lower_groups, 0)
 
+
     for r in range(1, 16):
         o = (me + r) % 16
         send(ob.at[0], orecv.at[pl.ds(o * 4, 4)], o_ss.at[tile_of(o)], o_rs.at[o], member(o)).wait_recv()
@@ -422,7 +418,7 @@
     for p in range(HEADS):
         out_ref[:, p * HD : (p + 1) * HD] = orecv[order_ref[p]]
 
-    for r in range(1, 8):
+    for r in range(7):
         send(kvs.at[0], kv.at[here], a_ss.at[r], a_rs.at[0], twin).wait_send()
     for r in range(1, 16):
         o = (me + r) % 16

time: 154 us -> 144 us (0.935); the launches traced: 154 us -> 142 us
  Pallas kernels: 150 us -> 138 us
    pallas_call x1, Pallas kernels: 150 us -> 138 us  [body(): pl.pallas_call(kernel, out_shape=jax.ShapeDtypeStruct((TILE, HEADS * HD),...]
where the time goes in v3:
time: 144 us; the launch traced here: 142 us
  Pallas kernels  138 us (96%)
  local copies, waits for them, and re-layouts  4.49 us (3%)
    pallas_call x1, Pallas kernels, body(): pl.pallas_call(kernel, out_shape=jax.ShapeDtypeStruct((TILE, HEADS * HD),...  138 us
    unnamed x2, local copies, waits for them, and re-layouts  4.49 us

profile of v3, /device:TPU:31, one launch (start us, length us, event | category | flops | bytes accessed | tf_op | source)
XLA Modules:
  0.0 142.4 jit_solution(15393999310002208666)
XLA Ops:
  0.0 1.4 copy.7.vert_ref
  1.4 137.9 %attention.1 = bf16[128,8192]{1,0:T(8,128)(2,1)} custom-call(s32[64]{0:T(128)} %band_ref.1, s32[64,16]{1,0:T(8,128)} %copy.7.vert_ref, s32[64]{0:T(128)} %order_ref.1, bf16[128,8192]{1,0:T(8,128)(2,1)} %q_ref.1, bf16[128,1024]{1,0:T(8,128)(2,1)} %k_ref.1, bf16[128,1024]{1,0:T(8,128)(2,1)} %v_ref.1), custom_call_target="tpu_custom_call" | custom-call | tf_op jit(solution)/shard_map/attention/pallas_call | solution.py:460
  139.3 3.1 %copy.9 = bf16[128,8192]{1,0:T(8,128)(2,1)} copy(bf16[128,8192]{1,0:T(8,128)(2,1)} %attention.1) | data formatting | bytes 4194304

commit v4 on v3

--- a/solution.py
+++ b/solution.py
@@ -294,10 +294,18 @@
     def queries_of(mi):
         return [qb[mi, :, rows[a]] for a in range(4)]
 
+    def turn(pos):
+        u, col = pos // 4, (x + (1 + 2 * (pos % 4)) % 5) % 4
+        core = (u // 2 + (4 - col) // 4) % 2
+        dy = (u + ((col + 1) // 2) % 2) % 2
+        return col * 4 + core * 2 + (yhi + dy) % 2
+
+    def send_turn(pos, carry):
+        send_out(turn(pos))
+        return carry
+
     def attend_lower_groups(pos, carry):
-        dx, u = (1 + 2 * (pos % 4)) % 5, pos // 4
-        dc, dy = ((u + 1) // 2) % 2, 1 - u // 2
-        mi = (((x + dx) % 4) * 2 + (c + dc) % 2) * 2 + (yhi + dy) % 2
+        mi = turn(pos)
         t, _ = place(mi)
         qs = queries_of(mi)
         for ch in range(2):
@@ -397,19 +405,24 @@
         def _():
             for a in range(4):
                 ob[mi, a] = (acc1[mi, rows[a], :] / den1[mi, rows[a], :]).astype(bf)
-            send_out(mi)
+
+        @pl.when(lower & (it >= 12))
+        def _():
+            lax.fori_loop(4 * (it - 12), 4 * (it - 11), send_turn, 0)
+
+        @pl.when(upper & (it == 12))
+        def _():
+            for n in range(4):
+                for d in (PLUS, MINUS):
+                    share(n, d, 1 - z % 2).wait_recv()
+
+        @pl.when(upper & (it >= 12))
+        def _():
+            lax.fori_loop(4 * (it - 12), 4 * (it - 11), attend_lower_groups, 0)
 
         return carry
 
     lax.fori_loop(0, 16, attend, 0)
-
-    @pl.when(upper)
-    def _():
-        for n in range(4):
-            for d in (PLUS, MINUS):
-                share(n, d, 1 - z % 2).wait_recv()
-        lax.fori_loop(0, 16, attend_lower_groups, 0)
-
 
     for r in range(1, 16):
         o = (me + r) % 16

time: 144 us -> 134 us (0.931)
  Pallas kernels: 138 us -> 128 us
    pallas_call x1, Pallas kernels: 138 us -> 128 us  [body(): pl.pallas_call(kernel, out_shape=jax.ShapeDtypeStruct((TILE, HEADS * HD),...]
where the time goes in v4:
time: 134 us; the launch traced here: 132 us
  Pallas kernels  128 us (96%)
  local copies, waits for them, and re-layouts  4.49 us (3%)
    pallas_call x1, Pallas kernels, body(): pl.pallas_call(kernel, out_shape=jax.ShapeDtypeStruct((TILE, HEADS * HD),...  128 us
    unnamed x2, local copies, waits for them, and re-layouts  4.49 us

profile of v4, /device:TPU:31, one launch (start us, length us, event | category | flops | bytes accessed | tf_op | source)
XLA Modules:
  0.0 132.4 jit_solution(3975656709591092543)
XLA Ops:
  0.0 1.4 %copy.7.vert_ref = s32[64,16]{1,0:T(8,128)} copy(s32[64,16]{0,1:T(8,128)} %param.10) | data formatting | bytes 8192 | tf_op args[4]
  1.4 127.9 %attention.1 = bf16[128,8192]{1,0:T(8,128)(2,1)} custom-call(s32[64]{0:T(128)} %band_ref.1, s32[64,16]{1,0:T(8,128)} %copy.7.vert_ref, s32[64]{0:T(128)} %order_ref.1, bf16[128,8192]{1,0:T(8,128)(2,1)} %q_ref.1, bf16[128,1024]{1,0:T(8,128)(2,1)} %k_ref.1, bf16[128,1024]{1,0:T(8,128)(2,1)} %v_ref.1), custom_call_target="tpu_custom_call" | custom-call | tf_op jit(solution)/shard_map/attention/pallas_call | solution.py:473
  129.3 3.1 %copy.9 = bf16[128,8192]{1,0:T(8,128)(2,1)} copy(bf16[128,8192]{1,0:T(8,128)(2,1)} %attention.1) | data formatting | bytes 4194304

commit v5 on v4

--- a/solution.py
+++ b/solution.py
@@ -406,9 +406,9 @@
             for a in range(4):
                 ob[mi, a] = (acc1[mi, rows[a], :] / den1[mi, rows[a], :]).astype(bf)
 
-        @pl.when(lower & (it >= 12))
-        def _():
-            lax.fori_loop(4 * (it - 12), 4 * (it - 11), send_turn, 0)
+        @pl.when(lower & (it >= 14))
+        def _():
+            lax.fori_loop(8 * (it - 14), 8 * (it - 13), send_turn, 0)
 
         @pl.when(upper & (it == 12))
         def _():

time: 134 us -> 134 us (level)
  no operation moved by 1% of the time
where the time goes in v5:
time: 134 us; the launch traced here: 132 us
  Pallas kernels  128 us (96%)
  local copies, waits for them, and re-layouts  4.49 us (3%)
    pallas_call x1, Pallas kernels, body(): pl.pallas_call(kernel, out_shape=jax.ShapeDtypeStruct((TILE, HEADS * HD),...  128 us
    unnamed x2, local copies, waits for them, and re-layouts  4.49 us

profile of v5, /device:TPU:31, one launch (start us, length us, event | category | flops | bytes accessed | tf_op | source)
XLA Modules:
  0.0 132.4 jit_solution(12788041471616280776)
XLA Ops:
  0.0 1.4 %copy.7.vert_ref = s32[64,16]{1,0:T(8,128)} copy(s32[64,16]{0,1:T(8,128)} %param.10) | data formatting | bytes 8192 | tf_op args[4]
  1.4 127.9 %attention.1 = bf16[128,8192]{1,0:T(8,128)(2,1)} custom-call(s32[64]{0:T(128)} %band_ref.1, s32[64,16]{1,0:T(8,128)} %copy.7.vert_ref, s32[64]{0:T(128)} %order_ref.1, bf16[128,8192]{1,0:T(8,128)(2,1)} %q_ref.1, bf16[128,1024]{1,0:T(8,128)(2,1)} %k_ref.1, bf16[128,1024]{1,0:T(8,128)(2,1)} %v_ref.1), custom_call_target="tpu_custom_call" | custom-call | tf_op jit(solution)/shard_map/attention/pallas_call | solution.py:473
  129.3 3.1 %copy.9 = bf16[128,8192]{1,0:T(8,128)(2,1)} copy(bf16[128,8192]{1,0:T(8,128)(2,1)} %attention.1) | data formatting | bytes 4194304
